TPU v7x, 32 devices: a whole 2x2x4 slice. The times are simulated.
32 devices in a mesh: dp: 8 (over z, y), seq: 4 (over x, core).
Axes of the slice: x: 2, y: 2, z: 4, core: 2. Of those that a mesh axis runs over, the one named last changes fastest.
Arguments:
- long_input: bfloat16 [8, 2048, 768], P('dp', 'seq'), may hold values from -6 to 6
- global_input: bfloat16 [8, 230, 768], P('dp'), may hold values from -6 to 6
- lengths: int32 [8], P('dp'), may hold values from 1024 to 2048, as said below
- w_query: bfloat16 [768, 768], replicated, may hold values from -0.21875 to 0.21875
- b_query: float32 [768], replicated, may hold values from -1.25 to 1.25
- w_key: bfloat16 [768, 768], replicated, may hold values from -0.21875 to 0.21875
- w_value: bfloat16 [768, 768], replicated, may hold values from -0.21875 to 0.21875
- b_value: float32 [768], replicated, may hold values from -1.25 to 1.25
- w_out: bfloat16 [768, 768], replicated, may hold values from -6 to 6
- b_out: float32 [768], replicated, may hold values from -1.25 to 1.25
- w_inner: bfloat16 [768, 3072], replicated, may hold values from -0.21875 to 0.21875
- b_inner: float32 [3072], replicated, may hold values from -1.25 to 1.25
- w_outer: bfloat16 [3072, 768], replicated, may hold values from -0.109375 to 0.109375
- b_outer: float32 [768], replicated, may hold values from -1.25 to 1.25
- norm1_gain: float32 [768], replicated, may hold values from 0.5 to 1.5
- norm1_shift: float32 [768], replicated, may hold values from -1.25 to 1.25
- norm2_gain: float32 [768], replicated, may hold values from 0.5 to 1.5
- norm2_shift: float32 [768], replicated, may hold values from -1.25 to 1.25
- rel_table: float32 [169, 12], replicated, may hold values from -6 to 6
- long_cotangent: bfloat16 [8, 2048, 768], P('dp', 'seq'), may hold values from -6 to 6
- global_cotangent: bfloat16 [8, 230, 768], P('dp'), may hold values from -6 to 6
Outputs:
- long_output: bfloat16 [8, 2048, 768], P('dp', 'seq')
- global_output: bfloat16 [8, 230, 768], P('dp')
- long_grad: float32 [8, 2048, 768], P('dp', 'seq')
- global_grad: float32 [8, 230, 768], P('dp')
- grad_w_query: float32 [768, 768], P(('dp', 'seq'))
- grad_b_query: float32 [768], P(('dp', 'seq'))
- grad_w_key: float32 [768, 768], P(('dp', 'seq'))
- grad_w_value: float32 [768, 768], P(('dp', 'seq'))
- grad_b_value: float32 [768], P(('dp', 'seq'))
- grad_w_out: float32 [768, 768], P(('dp', 'seq'))
- grad_b_out: float32 [768], P(('dp', 'seq'))
- grad_w_inner: float32 [768, 3072], P(('dp', 'seq'))
- grad_b_inner: float32 [3072], P(('dp', 'seq'))
- grad_w_outer: float32 [3072, 768], P(('dp', 'seq'))
- grad_b_outer: float32 [768], P(('dp', 'seq'))
- grad_norm1_gain: float32 [768], P(('dp', 'seq'))
- grad_norm1_shift: float32 [768], P(('dp', 'seq'))
- grad_norm2_gain: float32 [768], P(('dp', 'seq'))
- grad_norm2_shift: float32 [768], P(('dp', 'seq'))
- grad_rel_table: float32 [169, 12], replicated
Inputs may be any that keep to these rules, and one draw needn't show every extreme that they name: `lengths`: true long-token count of each document, whose long slots from it up to 2048 are padding; some document has all 2048 slots valid.
All inputs are finite; a program needn't handle non-finite values.
Results may differ from a plain program's by a relative error of at most 0.015.
Values may be sent and summed in bfloat16 or wider, within the bound.
A program may use at most 256 MiB of HBM per device.

v0:
```python
import jax
import jax.numpy as jnp
from jax import lax
from jax.sharding import PartitionSpec as P

HD = 64
R = 84
QB = 512
SB = 128


EPSILON = 1e-05
MASKED = -1e30


def padded_2(block, sides, width):
    for axis, dim in sides:
        count = lax.axis_size(axis)
        forward = [(i, i + 1) for i in range(count - 1)]
        backward = [(target, source) for source, target in forward]
        low = lax.ppermute(
            lax.slice_in_dim(block, block.shape[dim] - width, None, axis=dim), axis, forward
        )
        high = lax.ppermute(lax.slice_in_dim(block, 0, width, axis=dim), axis, backward)
        block = jnp.concatenate([low, block, high], axis=dim)
    return block


def combined_all(part, axis, combine):
    gathered = jax.tree.map(lambda a: lax.all_gather(a, axis), part)

    def take(source):
        return jax.tree.map(lambda a: lax.dynamic_index_in_dim(a, source, 0, False), gathered)

    return lax.fori_loop(
        1, lax.axis_size(axis), lambda source, state: combine(state, take(source)), take(0)
    )


def passed_along(value, axis, steps):
    count = lax.axis_size(axis)
    first, last = (max(0, -steps), min(count, count - steps))
    return lax.ppermute(value, axis, [(source, source + steps) for source in range(first, last)])


def split_up(x, dim, devices):
    before, after = (x.shape[:dim], x.shape[dim + 1 :])
    return jnp.moveaxis(x.reshape(*before, devices, -1, *after), dim, 0)


def sent_and_summed(x, axis, dim):
    parts = split_up(x, dim, lax.axis_size(axis))
    arrived = lax.all_to_all(parts, axis, split_axis=0, concat_axis=0, tiled=True)
    return arrived.astype(jnp.float32).sum(axis=0)


def in_one_piece(arrays, axis, dim, along):
    columns = [a.reshape(*a.shape[:along], -1) for a in arrays]
    both = jnp.concatenate(columns, axis=along)
    filled, at, done = (sent_and_summed(both, axis, dim), 0, [])
    for a, column in zip(arrays, columns):
        slab = filled[..., at : at + column.shape[along]]
        done.append(slab.reshape(*slab.shape[:along], *a.shape[along:]))
        at += column.shape[along]
    return tuple(done)


def norm_forward(values, gain, shift):
    average = jnp.mean(values, -1, keepdims=True)
    centred = values - average
    variance = jnp.mean(centred * centred, -1, keepdims=True)
    inverse = lax.rsqrt(variance + EPSILON)
    normed = centred * inverse
    return (normed * gain + shift, normed, inverse)


def norm_backward(grad_rows, normed, inverse, gain, row_weight):
    scaled = grad_rows * gain
    grad_in = inverse * (
        scaled
        - jnp.mean(scaled, -1, keepdims=True)
        - normed * jnp.mean(scaled * normed, -1, keepdims=True)
    )
    return (
        grad_in,
        jnp.sum(row_weight * grad_rows * normed, 0),
        jnp.sum(row_weight * grad_rows, 0),
    )


def split_heads(matrix):
    return matrix.reshape(matrix.shape[0], -1, HD)


def spread_diag(diag_values, width):
    row_count = diag_values.shape[-2]
    lead = [(0, 0)] * (diag_values.ndim - 1)
    padded = jnp.pad(diag_values, lead + [(0, width + 1 - diag_values.shape[-1])])
    flattened = padded.reshape(diag_values.shape[:-2] + (row_count * (width + 1),))
    return flattened[..., : row_count * width].reshape(diag_values.shape[:-2] + (row_count, width))


def collect_diag(full_rows, label_count):
    row_count, width = (full_rows.shape[-2], full_rows.shape[-1])
    flattened = full_rows.reshape(full_rows.shape[:-2] + (row_count * width,))
    flattened = jnp.pad(flattened, [(0, 0)] * (flattened.ndim - 1) + [(0, row_count)])
    return flattened.reshape(full_rows.shape[:-2] + (row_count, width + 1))[..., :label_count]


def smooth_gate(values):
    return jax.nn.gelu(values, approximate=True)


def combine_parts(earlier, later):
    joined_max = jnp.maximum(earlier[0], later[0])
    return (
        joined_max,
        earlier[1] * jnp.exp(earlier[0] - joined_max) + later[1] * jnp.exp(later[0] - joined_max),
    )


def heads_dot(left, right):
    return jnp.einsum("qhd,khd->hqk", left, right, preferred_element_type=jnp.float32)


def probs_dot(probabilities, values):
    return jnp.einsum("hqk,khd->qhd", probabilities, values, preferred_element_type=jnp.float32)


def keys_dot(probabilities, queries):
    return jnp.einsum("hqk,qhd->khd", probabilities, queries, preferred_element_type=jnp.float32)


def rows_dot(left, right):
    return jnp.einsum("rd,re->de", left, right, preferred_element_type=jnp.float32)


def regroup(member, data_count, seq_count):
    piece_rows = member.shape[0] // (data_count * seq_count)
    shaped = member.reshape((data_count, seq_count, piece_rows) + member.shape[1:])
    return jnp.swapaxes(shaped, 0, 1).reshape(member.shape)


def on_device(
    long_input,
    global_input,
    lengths,
    w_query,
    b_query,
    w_key,
    w_value,
    b_value,
    w_out,
    b_out,
    w_inner,
    b_inner,
    w_outer,
    b_outer,
    norm1_gain,
    norm1_shift,
    norm2_gain,
    norm2_shift,
    rel_table,
    long_cotangent,
    global_cotangent,
):
    f32 = jnp.float32
    bf16 = jnp.bfloat16
    seq_count = lax.axis_size("seq")
    seq_index = lax.axis_index("seq")
    block_len = long_input.shape[1]
    glob_count = global_input.shape[1]
    width_model = long_input.shape[2]
    head_count = rel_table.shape[1]
    score_scale = HD ** (-0.5)
    label_count = 2 * R + 1
    sub_count = QB // SB
    sub_window = SB + 2 * R
    doc_len = lengths[0]
    positions = seq_index * block_len + jnp.arange(block_len, dtype=jnp.int32)
    row_valid = positions < doc_len
    key_pos = seq_index * block_len - R + jnp.arange(block_len + 2 * R, dtype=jnp.int32)
    key_valid = (key_pos >= 0) & (key_pos < doc_len)
    owner_mask = (jnp.arange(glob_count) % seq_count == seq_index).astype(f32)[:, None]
    row_weight = jnp.concatenate([jnp.ones((block_len, 1), f32), owner_mask], 0)
    weight_low = row_weight.astype(bf16)
    whole_x = jnp.concatenate([long_input[0].astype(f32), global_input[0].astype(f32)], 0)
    normed_one, hat_one, inv_one = norm_forward(whole_x, norm1_gain, norm1_shift)
    normed_low = normed_one.astype(bf16)
    queries = (jnp.dot(normed_low, w_query, preferred_element_type=f32) + b_query).astype(bf16)
    keys = jnp.dot(normed_low, w_key, preferred_element_type=f32).astype(bf16)
    values = (jnp.dot(normed_low, w_value, preferred_element_type=f32) + b_value).astype(bf16)
    long_q = queries[:block_len]
    long_k = keys[:block_len]
    long_v = values[:block_len]
    glob_q_heads = split_heads(queries[block_len:])
    glob_k_heads = split_heads(keys[block_len:])
    glob_v_heads = split_heads(values[block_len:])
    own_k_heads = split_heads(long_k)
    own_v_heads = split_heads(long_v)
    table_heads = jnp.broadcast_to(rel_table.T[:, None, :], (head_count, SB, label_count))
    band_bias = spread_diag(table_heads, sub_window)
    band_mask = spread_diag(jnp.ones((SB, label_count), f32), sub_window) > 0.5
    extended = padded_2(jnp.stack([long_k, long_v]), (("seq", 1),), R)

    def band_block(row_start):
        query_blk = split_heads(long_q).reshape(sub_count, SB, head_count, HD)
        starts = [row_start + sub_index * SB for sub_index in range(sub_count)]
        key_win = jnp.stack(
            [split_heads(extended[0, begin : begin + sub_window]) for begin in starts]
        )
        value_win = jnp.stack(
            [split_heads(extended[1, begin : begin + sub_window]) for begin in starts]
        )
        valid_win = jnp.stack([key_valid[begin : begin + sub_window] for begin in starts])
        keep_mask = band_mask[None, None] & valid_win[:, None, None, :]
        raw_band = jnp.einsum("nqhd,nkhd->nhqk", query_blk, key_win, preferred_element_type=f32)
        band_scores = jnp.where(keep_mask, raw_band * score_scale + band_bias[None], MASKED)
        glob_scores = (
            jnp.einsum("nqhd,khd->nhqk", query_blk, glob_k_heads, preferred_element_type=f32)
            * score_scale
        )
        return (query_blk, key_win, value_win, keep_mask, band_scores, glob_scores)

    block_index = 0
    row_start = block_index * QB
    query_blk, key_win, value_win, keep_mask, band_scores, glob_scores = band_block(row_start)
    row_max = jnp.maximum(jnp.max(band_scores, -1), jnp.max(glob_scores, -1))
    band_exp = jnp.where(keep_mask, jnp.exp(band_scores - row_max[..., None]), 0.0)
    glob_exp = jnp.exp(glob_scores - row_max[..., None])
    denominator = jnp.sum(band_exp, -1) + jnp.sum(glob_exp, -1)
    attended = jnp.einsum(
        "nhqk,nkhd->nqhd",
        (band_exp / denominator[..., None]).astype(bf16),
        value_win,
        preferred_element_type=f32,
    ) + jnp.einsum(
        "nhqk,khd->nqhd",
        (glob_exp / denominator[..., None]).astype(bf16),
        glob_v_heads,
        preferred_element_type=f32,
    )
    attn_rows = [attended.reshape(QB, width_model)]
    long_norms = [row_max + jnp.log(denominator)]
    far_scores = jnp.where(
        row_valid[None, None, :], heads_dot(glob_q_heads, own_k_heads) * score_scale, MASKED
    )
    part_max = jnp.max(far_scores, -1)
    part_total = jnp.sum(
        jnp.where(row_valid[None, None, :], jnp.exp(far_scores - part_max[..., None]), 0.0), -1
    )
    far_max, far_total = combined_all((part_max, part_total), "seq", combine_parts)
    near_scores = heads_dot(glob_q_heads, glob_k_heads) * score_scale
    glob_max = jnp.maximum(far_max, jnp.max(near_scores, -1))
    glob_total = far_total * jnp.exp(far_max - glob_max) + jnp.sum(
        jnp.exp(near_scores - glob_max[..., None]), -1
    )
    glob_norm = glob_max + jnp.log(glob_total)
    far_probs = jnp.where(row_valid[None, None, :], jnp.exp(far_scores - glob_norm[..., None]), 0.0)
    near_probs = jnp.exp(near_scores - glob_norm[..., None])
    far_probs_low = far_probs.astype(bf16)
    near_probs_low = near_probs.astype(bf16)
    far_sum = lax.psum(probs_dot(far_probs_low, own_v_heads).astype(jnp.bfloat16), "seq").astype(
        jnp.float32
    )
    glob_attn = (far_sum + probs_dot(near_probs_low, glob_v_heads)).reshape(glob_count, width_model)
    attn_low = jnp.concatenate(attn_rows + [glob_attn], 0).astype(bf16)
    residual_mid = whole_x + jnp.dot(attn_low, w_out, preferred_element_type=f32) + b_out
    normed_two, hat_two, inv_two = norm_forward(residual_mid, norm2_gain, norm2_shift)
    normed_two_low = normed_two.astype(bf16)
    hidden_pre = jnp.dot(normed_two_low, w_inner, preferred_element_type=f32) + b_inner
    activated, gelu_back = jax.vjp(smooth_gate, hidden_pre)
    activated_low = activated.astype(bf16)
    result = residual_mid + jnp.dot(activated_low, w_outer, preferred_element_type=f32) + b_outer
    long_result = jnp.where(row_valid[:, None], result[:block_len], 0.0).astype(bf16)
    glob_result = result[block_len:].astype(bf16)
    grad_y = jnp.concatenate(
        [
            long_cotangent[0].astype(f32) * row_valid[:, None].astype(f32),
            global_cotangent[0].astype(f32),
        ],
        0,
    )
    grad_b_outer = jnp.sum(grad_y * row_weight, 0)
    grad_y_low = grad_y.astype(bf16)
    grad_w_outer = rows_dot(activated_low, grad_y_low * weight_low)
    grad_act = jnp.dot(grad_y_low, w_outer.T, preferred_element_type=f32)
    (grad_hidden,) = gelu_back(grad_act)
    grad_b_inner = jnp.sum(grad_hidden * row_weight, 0)
    hidden_low = grad_hidden.astype(bf16)
    grad_w_inner = rows_dot(normed_two_low, hidden_low * weight_low)
    grad_normed_two = jnp.dot(hidden_low, w_inner.T, preferred_element_type=f32)
    grad_from_two, grad_gain_two, grad_shift_two = norm_backward(
        grad_normed_two, hat_two, inv_two, norm2_gain, row_weight
    )
    grad_mid = grad_y + grad_from_two
    grad_b_out = jnp.sum(grad_mid * row_weight, 0)
    grad_mid_low = grad_mid.astype(bf16)
    grad_w_out = rows_dot(attn_low, grad_mid_low * weight_low)
    grad_attn_low = jnp.dot(grad_mid_low, w_out.T, preferred_element_type=f32).astype(bf16)
    long_grad_o = split_heads(grad_attn_low[:block_len])
    glob_grad_o = split_heads(grad_attn_low[block_len:])
    ext_grad = jnp.zeros((2, block_len + 2 * R, width_model), f32)
    block_index = 0
    row_start = block_index * QB
    query_blk, key_win, value_win, keep_mask, band_scores, glob_scores = band_block(row_start)
    log_norm = long_norms[block_index][..., None]
    band_probs = jnp.where(keep_mask, jnp.exp(band_scores - log_norm), 0.0)
    glob_probs = jnp.exp(glob_scores - log_norm)
    grad_o = long_grad_o.reshape(sub_count, SB, head_count, HD)
    band_dp = jnp.einsum("nqhd,nkhd->nhqk", grad_o, value_win, preferred_element_type=f32)
    glob_dp = jnp.einsum("nqhd,khd->nhqk", grad_o, glob_v_heads, preferred_element_type=f32)
    row_delta = jnp.sum(band_probs * band_dp, -1) + jnp.sum(glob_probs * glob_dp, -1)
    band_ds = band_probs * (band_dp - row_delta[..., None])
    glob_ds = glob_probs * (glob_dp - row_delta[..., None])
    table_grad = jnp.sum(collect_diag(band_ds, label_count), (0, 2))
    band_ds_low = band_ds.astype(bf16)
    glob_ds_low = glob_ds.astype(bf16)
    grad_query = (
        jnp.einsum("nhqk,nkhd->nqhd", band_ds_low, key_win, preferred_element_type=f32)
        + jnp.einsum("nhqk,khd->nqhd", glob_ds_low, glob_k_heads, preferred_element_type=f32)
    ) * score_scale
    query_grads = [grad_query.reshape(QB, width_model)]
    grad_key_win = (
        jnp.einsum("nhqk,nqhd->nkhd", band_ds_low, query_blk, preferred_element_type=f32)
        * score_scale
    )
    grad_value_win = jnp.einsum(
        "nhqk,nqhd->nkhd", band_probs.astype(bf16), grad_o, preferred_element_type=f32
    )
    for sub_index in range(sub_count):
        begin = row_start + sub_index * SB
        ext_grad = ext_grad.at[0, begin : begin + sub_window].add(
            grad_key_win[sub_index].reshape(sub_window, width_model)
        )
        ext_grad = ext_grad.at[1, begin : begin + sub_window].add(
            grad_value_win[sub_index].reshape(sub_window, width_model)
        )
    glob_key_part = (
        jnp.einsum("nhqk,nqhd->khd", glob_ds_low, query_blk, preferred_element_type=f32)
        * score_scale
    )
    glob_value_part = jnp.einsum(
        "nhqk,nqhd->khd", glob_probs.astype(bf16), grad_o, preferred_element_type=f32
    )
    far_dp = heads_dot(glob_grad_o, own_v_heads)
    near_dp = heads_dot(glob_grad_o, glob_v_heads)
    far_delta = lax.psum(jnp.sum(far_probs * far_dp, -1), "seq")
    glob_delta = far_delta + jnp.sum(near_probs * near_dp, -1)
    far_ds_low = (far_probs * (far_dp - glob_delta[..., None])).astype(bf16)
    near_ds_low = (near_probs * (near_dp - glob_delta[..., None])).astype(bf16)
    glob_query_part = probs_dot(far_ds_low, own_k_heads) * score_scale
    own_key_grad = keys_dot(far_ds_low, glob_q_heads) * score_scale
    own_value_grad = keys_dot(far_probs_low, glob_grad_o)
    summed = (
        lax.psum(glob_query_part.astype(jnp.bfloat16), "seq").astype(jnp.float32),
        lax.psum(glob_key_part.astype(jnp.bfloat16), "seq").astype(jnp.float32),
        lax.psum(glob_value_part.astype(jnp.bfloat16), "seq").astype(jnp.float32),
    )
    glob_grad_q = summed[0] + probs_dot(near_ds_low, glob_k_heads) * score_scale
    glob_grad_k = summed[1] + keys_dot(near_ds_low, glob_q_heads) * score_scale
    glob_grad_v = summed[2] + keys_dot(near_probs_low, glob_grad_o)
    from_above = passed_along(ext_grad[:, :R].astype(jnp.bfloat16), "seq", -1).astype(jnp.float32)
    from_below = passed_along(ext_grad[:, R + block_len :].astype(jnp.bfloat16), "seq", 1).astype(
        jnp.float32
    )
    own_grad = ext_grad[:, R : R + block_len]
    own_grad = own_grad.at[:, :R].add(from_below)
    own_grad = own_grad.at[:, block_len - R :].add(from_above)
    long_grad_k = own_grad[0] + own_key_grad.reshape(block_len, width_model)
    long_grad_v = own_grad[1] + own_value_grad.reshape(block_len, width_model)
    query_low = jnp.concatenate(
        query_grads + [glob_grad_q.reshape(glob_count, width_model)], 0
    ).astype(bf16)
    key_low = jnp.concatenate(
        [long_grad_k, glob_grad_k.reshape(glob_count, width_model)], 0
    ).astype(bf16)
    value_low = jnp.concatenate(
        [long_grad_v, glob_grad_v.reshape(glob_count, width_model)], 0
    ).astype(bf16)
    grad_b_query = jnp.sum(query_low.astype(f32) * row_weight, 0)
    grad_b_value = jnp.sum(value_low.astype(f32) * row_weight, 0)
    grad_w_query = rows_dot(normed_low, query_low * weight_low)
    grad_w_key = rows_dot(normed_low, key_low * weight_low)
    grad_w_value = rows_dot(normed_low, value_low * weight_low)
    grad_normed_one = (
        jnp.dot(query_low, w_query.T, preferred_element_type=f32)
        + jnp.dot(key_low, w_key.T, preferred_element_type=f32)
        + jnp.dot(value_low, w_value.T, preferred_element_type=f32)
    )
    grad_from_one, grad_gain_one, grad_shift_one = norm_backward(
        grad_normed_one, hat_one, inv_one, norm1_gain, row_weight
    )
    grad_x = grad_mid + grad_from_one
    data_count = lax.axis_size("dp")
    seq_part = (
        lax.psum_scatter(
            regroup(grad_w_query, data_count, seq_count).astype(jnp.bfloat16),
            "seq",
            scatter_dimension=0,
            tiled=True,
        ).astype(jnp.float32),
        lax.psum_scatter(
            regroup(grad_b_query, data_count, seq_count).astype(jnp.bfloat16),
            "seq",
            scatter_dimension=0,
            tiled=True,
        ).astype(jnp.float32),
        lax.psum_scatter(
            regroup(grad_w_key, data_count, seq_count).astype(jnp.bfloat16),
            "seq",
            scatter_dimension=0,
            tiled=True,
        ).astype(jnp.float32),
        lax.psum_scatter(
            regroup(grad_w_value, data_count, seq_count).astype(jnp.bfloat16),
            "seq",
            scatter_dimension=0,
            tiled=True,
        ).astype(jnp.float32),
        lax.psum_scatter(
            regroup(grad_b_value, data_count, seq_count).astype(jnp.bfloat16),
            "seq",
            scatter_dimension=0,
            tiled=True,
        ).astype(jnp.float32),
        lax.psum_scatter(
            regroup(grad_w_out, data_count, seq_count).astype(jnp.bfloat16),
            "seq",
            scatter_dimension=0,
            tiled=True,
        ).astype(jnp.float32),
        lax.psum_scatter(
            regroup(grad_b_out, data_count, seq_count).astype(jnp.bfloat16),
            "seq",
            scatter_dimension=0,
            tiled=True,
        ).astype(jnp.float32),
        lax.psum_scatter(
            regroup(grad_w_inner, data_count, seq_count).astype(jnp.bfloat16),
            "seq",
            scatter_dimension=0,
            tiled=True,
        ).astype(jnp.float32),
        lax.psum_scatter(
            regroup(grad_b_inner, data_count, seq_count).astype(jnp.bfloat16),
            "seq",
            scatter_dimension=0,
            tiled=True,
        ).astype(jnp.float32),
        lax.psum_scatter(
            regroup(grad_w_outer, data_count, seq_count).astype(jnp.bfloat16),
            "seq",
            scatter_dimension=0,
            tiled=True,
        ).astype(jnp.float32),
        lax.psum_scatter(
            regroup(grad_b_outer, data_count, seq_count).astype(jnp.bfloat16),
            "seq",
            scatter_dimension=0,
            tiled=True,
        ).astype(jnp.float32),
        lax.psum_scatter(
            regroup(grad_gain_one, data_count, seq_count).astype(jnp.bfloat16),
            "seq",
            scatter_dimension=0,
            tiled=True,
        ).astype(jnp.float32),
        lax.psum_scatter(
            regroup(grad_shift_one, data_count, seq_count).astype(jnp.bfloat16),
            "seq",
            scatter_dimension=0,
            tiled=True,
        ).astype(jnp.float32),
        lax.psum_scatter(
            regroup(grad_gain_two, data_count, seq_count).astype(jnp.bfloat16),
            "seq",
            scatter_dimension=0,
            tiled=True,
        ).astype(jnp.float32),
        lax.psum_scatter(
            regroup(grad_shift_two, data_count, seq_count).astype(jnp.bfloat16),
            "seq",
            scatter_dimension=0,
            tiled=True,
        ).astype(jnp.float32),
    )
    reduced = (
        *in_one_piece(
            (
                seq_part[0].astype(jnp.bfloat16),
                seq_part[1].astype(jnp.bfloat16),
                seq_part[2].astype(jnp.bfloat16),
                seq_part[3].astype(jnp.bfloat16),
                seq_part[4].astype(jnp.bfloat16),
                seq_part[5].astype(jnp.bfloat16),
                seq_part[6].astype(jnp.bfloat16),
                seq_part[7].astype(jnp.bfloat16),
            ),
            "dp",
            0,
            1,
        ),
        *in_one_piece(
            (seq_part[8].astype(jnp.bfloat16), seq_part[9].astype(jnp.bfloat16)), "dp", 0, 1
        ),
        sent_and_summed(seq_part[10].astype(jnp.bfloat16), "dp", 0),
        sent_and_summed(seq_part[11].astype(jnp.bfloat16), "dp", 0),
        sent_and_summed(seq_part[12].astype(jnp.bfloat16), "dp", 0),
        sent_and_summed(seq_part[13].astype(jnp.bfloat16), "dp", 0),
        sent_and_summed(seq_part[14].astype(jnp.bfloat16), "dp", 0),
    )
    table_total = lax.psum(table_grad.T, ("dp", "seq"))
    return (
        long_result[None],
        glob_result[None],
        grad_x[:block_len][None],
        grad_x[block_len:][None],
        reduced[0],
        reduced[1],
        reduced[2],
        reduced[3],
        reduced[4],
        reduced[5],
        reduced[6],
        reduced[7],
        reduced[8],
        reduced[9],
        reduced[10],
        reduced[11],
        reduced[12],
        reduced[13],
        reduced[14],
        table_total,
    )


def solution(mesh):
    return jax.shard_map(
        on_device,
        mesh=mesh,
        in_specs=(
            P("dp", "seq", None),
            P("dp", None, None),
            P("dp"),
            P(),
            P(),
            P(),
            P(),
            P(),
            P(),
            P(),
            P(),
            P(),
            P(),
            P(),
            P(),
            P(),
            P(),
            P(),
            P(),
            P("dp", "seq", None),
            P("dp", None, None),
        ),
        out_specs=(
            P("dp", "seq", None),
            P("dp", None, None),
            P("dp", "seq", None),
            P("dp", None, None),
            P(("dp", "seq"), None),
            P(("dp", "seq")),
            P(("dp", "seq"), None),
            P(("dp", "seq"), None),
            P(("dp", "seq")),
            P(("dp", "seq"), None),
            P(("dp", "seq")),
            P(("dp", "seq"), None),
            P(("dp", "seq")),
            P(("dp", "seq"), None),
            P(("dp", "seq")),
            P(("dp", "seq")),
            P(("dp", "seq")),
            P(("dp", "seq")),
            P(("dp", "seq")),
            P(),
        ),
        check_vma=False,
    )
```

profile of v0, /device:TPU:0, one launch (start us, length us, event | category | flops | bytes accessed | tf_op | source)
XLA Modules:
  0.0 663.2 jit_solution(3501094494371293787)
XLA Ops:
  39.2 7.5 %all-gather.3 = f32[4,12,230]{2,1,0:T(8,128)S(1)} all-gather(f32[1,12,230]{2,1,0:T(8,128)S(1)} %bitcast.410), channel_id=3, replica_groups=mesh['dp'=8,'seq'=4] {'seq'}, dimensions={0}, use_global_device_ids=true | all-gather | bytes 55200 | tf_op jit(solution)/shard_map/all_gather | solution.py:30
  142.2 6.6 %fusion.160 = f32[742,3072]{1,0:T(8,128)} fusion(bf16[768,3072]{1,0:T(8,128)(2,1)S(1)} %bitcast.423, f32[742,768]{1,0:T(8,128)S(1)} %get-tuple-element.472, f32[768]{0:T(1024)S(1)} %copy-done.128, f32[768]{0:T(1024)S(1)} %copy-done.102, f32[742]{0:T(1024)S(1)} %add_rsqrt_fusion, f32[742]{0:T(1024)S(1)} %broadcast_multiply_fusion.4), kind=kOutput, calls=%fused_computation.291 | convolution fusion | flops 3504044544 | bytes 16127792 | tf_op jit(solution)/shard_map/dot_general | solution.py:271
  148.9 12.1 %multiply_reduce_fusion = (bf16[3072]{0:T(1024)(128)(2,1)}, bf16[742,3072]{1,0:T(8,128)(2,1)S(1)}) fusion(f32[742]{0:T(1024)S(1)} %copy-done.108, f32[742,3072]{1,0:T(8,128)} %fusion.160, f32[3072]{0:T(1024)S(1)} %copy-done.119, bf16[3072,768]{1,0:T(8,128)(2,1)S(1)} %bitcast.425, f32[230,768]{1,0:T(8,128)S(1)} %copy-done.44, f32[512,768]{1,0:T(8,128)S(1)} %copy-done.28), kind=kOutput, calls=%fused_computation.13 | convolution fusion | flops 3555898368 | bytes 20695960 | tf_op jit(solution)/shard_map/dot_general | solution.py:287
  175.0 6.1 multiply_reduce_fusion.2
  185.3 10.3 %multiply_reduce_fusion.1 = (f32[4,12,128]{2,1,0:T(8,128)}, f32[4,12,128,296]{2,3,1,0:T(8,128)}) fusion(f32[4,12,128,296]{2,3,1,0:T(8,128)} %copy-done.5, f32[4,12,128]{2,1,0:T(8,128)S(1)} %get-tuple-element.417, pred[4,128,296]{1,2,0:T(8,128)(4,1)} %broadcast_and_fusion, bf16[1,296,12,64]{1,3,2,0:T(8,128)(2,1)} %bitcast.397, ...), kind=kOutput, calls=%fused_computation.16 | convolution fusion | flops 242780160 | bytes 17354752 | tf_op jit(solution)/shard_map/nqhd,nkhd->nhqk/dot_general | solution.py:311
  197.5 12.4 %psum.43 = f32[12,230]{1,0:T(8,128)S(1)} all-reduce(f32[12,230]{1,0:T(8,128)} %get-tuple-element.474), channel_id=1, replica_groups=mesh['dp'=8,'seq'=4] {'seq'}, use_global_device_ids=true, to_apply=%region_20.21 | all-reduce | flops 2760 | bytes 22080 | tf_op jit(solution)/shard_map/psum | solution.py:348
  225.5 9.7 %convolution_convert_fusion = bf16[3072,768]{1,0:T(8,128)(2,1)S(1)} fusion(bf16[742]{0:T(1024)(128)(2,1)S(1)} %copy-done.113, f32[230,768]{1,0:T(8,128)S(1)} %copy-done.45, f32[512,768]{1,0:T(8,128)} %convert_multiply_fusion, f32[742,3072]{1,0:T(8,128)} %fusion.160, f32[3072]{0:T(1024)S(1)} %copy-done.120), kind=kOutput, calls=%fused_computation.39 | convolution fusion | flops 3529767936 | bytes 16129484 | tf_op jit(solution)/shard_map/rd,re->de/dot_general | solution.py:135
  263.9 6.8 %subtract_multiply_fusion = f32[4,12,128,296]{2,3,1,0:T(8,128)S(1)} fusion(f32[4,12,128,296]{2,3,1,0:T(8,128)} %get-tuple-element.479, f32[4,12,128,296]{2,3,1,0:T(8,128)} %copy-done.5, f32[4,12,128]{2,1,0:T(8,128)S(1)} %copy-done.76, f32[4,12,128]{2,1,0:T(8,128)S(1)} %get-tuple-element.417, pred[4,128,296]{1,2,0:T(8,128)(4,1)S(1)} %copy-done.48), kind=kLoop, calls=%fused_computation.15 | loop fusion | flops 7274496 | bytes 22024192 | tf_op jit(solution)/shard_map/mul | solution.py:314
  270.7 6.0 fusion.66
  401.1 7.1 %convolution_convert_fusion.1 = bf16[768,3072]{1,0:T(8,128)(2,1)S(1)} fusion(bf16[742]{0:T(1024)(128)(2,1)S(1)} %copy-done.115, bf16[742,3072]{1,0:T(8,128)(2,1)} %copy-done.132, f32[742,768]{1,0:T(8,128)S(1)} %copy-done.19, f32[768]{0:T(1024)S(1)} %copy-done.129, f32[768]{0:T(1024)S(1)} %copy-done.103, f32[742]{0:T(1024)S(1)} %copy-done.91, ...), kind=kOutput, calls=%fused_computation.40 | convolution fusion | flops 3508683264 | bytes 11570428 | tf_op jit(solution)/shard_map/rd,re->de/dot_general | solution.py:135
  418.6 5.9 fusion.46
  425.5 13.3 %all-reduce.14 = (bf16[768]{0:T(1024)(128)(2,1)}, bf16[768]{0:T(1024)(128)(2,1)}, bf16[768]{0:T(1024)(128)(2,1)}, bf16[3072]{0:T(1024)(128)(2,1)S(1)}, bf16[768]...) all-reduce(bf16[768]{0:T(1024)(128)(2,1)S(1)} %convert_element_type, ...), channel_id=5, replica_groups=mesh['dp'=8,'seq'=4] {'seq'}, use_global_device_ids=true, to_apply=%region_32.33.clone | all-reduce | flops 9216 | bytes 36864
  439.6 5.9 all-to-all-start.2
  446.3 5.6 all-to-all-done.2
  456.0 5.6 all-to-all-done.3
  465.7 5.6 all-to-all-done.4
  495.0 8.9 %copy.397 = f32[4,12,128,296]{3,2,0,1:T(8,128)} copy(f32[4,12,128,296]{2,3,1,0:T(8,128)} %copy-done.1) | data formatting | bytes 14548992 | tf_op jit(solution)/shard_map/mul | solution.py:314
  504.0 11.8 %reshape.753 = f32[4,12,37888]{2,0,1:T(4,128)} reshape(f32[4,12,128,296]{3,2,0,1:T(8,128)} %copy.397) | data formatting | bytes 14548992 | tf_op jit(solution)/shard_map/reshape | solution.py:105
  515.8 7.3 %pad.56 = f32[4,12,38016]{2,0,1:T(4,128)} pad(f32[4,12,37888]{2,0,1:T(4,128)} %reshape.753, f32[]{:T(128)} %constant.375.clone.1), padding=0_0x0_0x0_128 | pad | bytes 14573572 | tf_op jit(solution)/shard_map/jit(_pad)/pad | solution.py:106
  523.1 12.4 %reshape.754 = f32[4,12,128,297]{3,2,0,1:T(8,128)} reshape(f32[4,12,38016]{2,0,1:T(4,128)} %pad.56) | data formatting | bytes 14598144 | tf_op jit(solution)/shard_map/reshape | solution.py:107
  538.9 40.7 %psum.47 = f32[169,12]{0,1:T(8,128)} all-reduce(f32[169,12]{0,1:T(8,128)S(1)} %bitcast.411), channel_id=1, replica_groups=mesh['dp'=8,'seq'=4] {'dp','seq'}, use_global_device_ids=true, to_apply=%region_62.63 | all-reduce | flops 2028 | bytes 16224 | tf_op jit(solution)/shard_map/psum | solution.py:513
  591.7 6.3 all-to-all-start
  598.1 11.5 %add_add_fusion.1 = bf16[742,768]{1,0:T(8,128)(2,1)S(1)} fusion(f32[742,768]{1,0:T(8,128)} %copy-done.18, bf16[3072,768]{1,0:T(8,128)(2,1)} %param.55, f32[768]{0:T(1024)S(1)} %copy-done.130, f32[742,3072]{1,0:T(8,128)} %fusion.160, f32[3072]{0:T(1024)S(1)} %copy-done.121), kind=kOutput, calls=%fused_computation.100 | convolution fusion | flops 3525699072 | bytes 17270784 | tf_op jit(solution)/shard_map/dot_general | solution.py:274
  621.6 29.9 %all-to-all-done = bf16[8,24,6147]{2,1,0:T(8,128)(2,1)} async-done(((bf16[8,24,6147]{2,1,0:T(8,128)(2,1)}), bf16[8,24,6147]{2,1,0:T(8,128)(2,1)}, u32[]{:S(2)}, u32[]{:S(2)}) %all-to-all-start) | async-done | bytes 2360480 | tf_op jit(solution)/shard_map/all_to_all | solution.py:53
  (573 shorter events, 389.1 us)
Async XLA Ops:
  7.3 97.1 %all-reduce.19.cloned.1.call-start = ((), (), s32[]{:S(2)}) async-start(), calls=%async_computation.13 | async-start | bytes 786432 | tf_op jit(solution)/shard_map/psum | solution.py:263
  17.0 90.7 %collective-permute-start = (bf16[2,84,768]{2,1,0:T(8,128)(2,1)}, bf16[2,84,768]{2,1,0:T(8,128)(2,1)}, u32[]{:S(2)}, u32[]{:S(2)}) collective-permute-start(bf16[2,84,768]{2,1,0:T(8,128)(2,1)} %get-tuple-element.439), channel_id=1, source_target_pairs={{0,1},{1,2},{2,3},{4,5},{5,6},{6,7},{8,9},{9,10},{10,11},{12,13},{... | collective-permute-start | bytes 774152 | tf_op jit(solution)/shard_map/ppermute | solution.py:21
  20.1 87.6 %collective-permute-start.1 = (bf16[2,84,768]{2,1,0:T(8,128)(2,1)}, bf16[2,84,768]{2,1,0:T(8,128)(2,1)}, u32[]{:S(2)}, u32[]{:S(2)}) collective-permute-start(bf16[2,84,768]{2,1,0:T(8,128)(2,1)} %get-tuple-element.440), channel_id=1, source_target_pairs={{1,0},{2,1},{3,2},{5,4},{6,5},{7,6},{9,8},{10,9},{11,10},{13,12},{... | collective-permute-start | bytes 774152 | tf_op jit(solution)/shard_map/ppermute | solution.py:24
  59.6 279.6 %all-reduce.21.cloned.1.call-start = ((), (), s32[]{:S(2)}) async-start(), calls=%async_computation.20 | async-start | bytes 2359296 | tf_op jit(solution)/shard_map/psum | solution.py:356
  77.3 47.4 %copy-start.9 = (bf16[4,128,12,64]{1,0,3,2:T(4,128)(2,1)}, bf16[4,128,12,64]{1,0,3,2:T(4,128)(2,1)S(1)}, u32[]{:S(2)}) copy-start(bf16[4,128,12,64]{1,0,3,2:T(4,128)(2,1)S(1)} %reshape_reshape.7) | copy-start | bytes 2359300
  140.0 26.0 %copy-start.18 = (f32[742,768]{1,0:T(8,128)}, f32[742,768]{1,0:T(8,128)S(1)}, u32[]{:S(2)}) copy-start(f32[742,768]{1,0:T(8,128)S(1)} %get-tuple-element.472) | copy-start | bytes 6838276
  140.1 26.0 %copy-start.84 = (f32[742]{0:T(1024)}, f32[742]{0:T(1024)S(1)}, u32[]{:S(2)}) copy-start(f32[742]{0:T(1024)S(1)} %broadcast_multiply_fusion.4) | copy-start | bytes 8908
  142.2 23.9 %copy-start.90 = (f32[742]{0:T(1024)}, f32[742]{0:T(1024)S(1)}, u32[]{:S(2)}) copy-start(f32[742]{0:T(1024)S(1)} %add_rsqrt_fusion) | copy-start | bytes 8908
  175.0 20.5 %slice-start.2 = ((s8[5701632]{0:T(1024)(128)(4,1)}), s8[1507328]{0:T(1024)(128)(4,1)S(1)}, s32[]{:S(2)}) async-start(s8[5701632]{0:T(1024)(128)(4,1)} %bitcast.309), calls=%async_computation.23 | async-start | bytes 3014656
  225.4 258.8 %reduce-scatter.17.cloned.1.call-start = ((), (), s32[]{:S(2)}) async-start(), calls=%async_computation.19 | async-start | bytes 5898240 | tf_op jit(solution)/shard_map/reduce_scatter | solution.py:451
  237.7 348.4 %reduce-scatter.13.cloned.1.call-start = ((), (), s32[]{:S(2)}) async-start(), calls=%async_computation.17 | async-start | bytes 1474560 | tf_op jit(solution)/shard_map/reduce_scatter | solution.py:427
  306.6 279.5 %reduce-scatter.7.cloned.1.call-start = ((), (), s32[]{:S(2)}) async-start(), calls=%async_computation.14 | async-start | bytes 1474560 | tf_op jit(solution)/shard_map/reduce_scatter | solution.py:397
  347.5 238.6 %reduce-scatter.11.cloned.1.call-start = ((), (), s32[]{:S(2)}) async-start(), calls=%async_computation.16 | async-start | bytes 1474560 | tf_op jit(solution)/shard_map/reduce_scatter | solution.py:415
  360.8 10.0 %collective-permute-start.2 = (bf16[2,84,768]{2,1,0:T(8,128)(2,1)S(1)}, bf16[2,84,768]{2,1,0:T(8,128)(2,1)}, u32[]{:S(2)}, u32[]{:S(2)}) collective-permute-start(bf16[2,84,768]{2,1,0:T(8,128)(2,1)S(1)} %get-tuple-element.432), channel_id=1, source_target_pairs={{0,1},{1,2},{2,3},{4,5},{5,6},{6,7},{8,9},{9,10},{10,11},{12,13},{... | collective-permute-start | bytes 774152 | tf_op jit(solution)/shard_map/ppermute | solution.py:43
  369.5 6.0 collective-permute-start.3
  391.6 194.5 %reduce-scatter.9.cloned.1.call-start = ((), (), s32[]{:S(2)}) async-start(), calls=%async_computation.15 | async-start | bytes 1474560 | tf_op jit(solution)/shard_map/reduce_scatter | solution.py:409
  400.2 185.9 %reduce-scatter.15.cloned.1.call-start = ((), (), s32[]{:S(2)}) async-start(), calls=%async_computation.18 | async-start | bytes 5898240 | tf_op jit(solution)/shard_map/reduce_scatter | solution.py:439
  439.6 12.3 %all-to-all-start.2 = ((bf16[8,1,24]{2,1,0:T(2,128)(2,1)}), bf16[8,1,24]{2,1,0:T(2,128)(2,1)S(1)}, u32[]{:S(2)}, u32[]{:S(2)}) async-start(bf16[8,1,24]{2,1,0:T(2,128)(2,1)} %all_to_all.48), calls=%async_computation.8 | async-start | bytes 8192 | tf_op jit(solution)/shard_map/all_to_all | solution.py:53
  451.9 9.6 %all-to-all-start.3 = ((bf16[8,1,24]{2,1,0:T(2,128)(2,1)}), bf16[8,1,24]{2,1,0:T(2,128)(2,1)S(1)}, u32[]{:S(2)}, u32[]{:S(2)}) async-start(bf16[8,1,24]{2,1,0:T(2,128)(2,1)} %all_to_all.49), calls=%async_computation.9 | async-start | bytes 8192 | tf_op jit(solution)/shard_map/all_to_all | solution.py:53
  461.6 9.6 %all-to-all-start.4 = ((bf16[8,1,24]{2,1,0:T(2,128)(2,1)}), bf16[8,1,24]{2,1,0:T(2,128)(2,1)S(1)}, u32[]{:S(2)}, u32[]{:S(2)}) async-start(bf16[8,1,24]{2,1,0:T(2,128)(2,1)} %all_to_all.50), calls=%async_computation.10 | async-start | bytes 8192 | tf_op jit(solution)/shard_map/all_to_all | solution.py:53
  471.2 9.6 %all-to-all-start.5 = ((bf16[8,1,24]{2,1,0:T(2,128)(2,1)}), bf16[8,1,24]{2,1,0:T(2,128)(2,1)S(1)}, u32[]{:S(2)}, u32[]{:S(2)}) async-start(bf16[8,1,24]{2,1,0:T(2,128)(2,1)} %all_to_all.51), calls=%async_computation.11 | async-start | bytes 8192 | tf_op jit(solution)/shard_map/all_to_all | solution.py:53
  480.9 9.6 %all-to-all-start.6 = ((bf16[8,1,24]{2,1,0:T(2,128)(2,1)}), bf16[8,1,24]{2,1,0:T(2,128)(2,1)S(1)}, u32[]{:S(2)}, u32[]{:S(2)}) async-start(bf16[8,1,24]{2,1,0:T(2,128)(2,1)} %all_to_all.52), calls=%async_computation.12 | async-start | bytes 8192 | tf_op jit(solution)/shard_map/all_to_all | solution.py:53
  490.5 101.2 %all-to-all-start.1 = ((bf16[8,96,769]{2,1,0:T(8,128)(2,1)}), bf16[8,96,769]{2,1,0:T(8,128)(2,1)}, u32[]{:S(2)}, u32[]{:S(2)}) async-start(bf16[8,96,769]{2,1,0:T(8,128)(2,1)} %pad_maximum_fusion.3), calls=%async_computation.7 | async-start | bytes 2752512 | tf_op jit(solution)/shard_map/all_to_all | solution.py:53
  591.7 59.7 %all-to-all-start = ((bf16[8,24,6147]{2,1,0:T(8,128)(2,1)}), bf16[8,24,6147]{2,1,0:T(8,128)(2,1)}, u32[]{:S(2)}, u32[]{:S(2)}) async-start(bf16[8,24,6147]{2,1,0:T(8,128)(2,1)} %concatenate.122), calls=%async_computation.5 | async-start | bytes 4816896 | tf_op jit(solution)/shard_map/all_to_all | solution.py:53
  (139 other events, 567.6 us)
Sparse Core Ops, SparseCore 0:
  59.8 34.0 all-reduce.18
  225.5 38.0 all-reduce.20
  266.3 47.8 reduce-scatter.16
  316.6 25.7 reduce-scatter.12
  347.6 26.0 reduce-scatter.6
  391.7 28.5 reduce-scatter.10
  423.0 25.7 reduce-scatter.8
  451.3 47.8 reduce-scatter.14
where the time goes:
time: 675 us; the launch traced here: 663 us
  local copies, waits for them, and re-layouts  216 us (32%)
  matrix products  170 us (25%)
  other arithmetic  87.2 us (13%)
  blocking collectives  79.5 us (12%)
  waiting for transfers between devices  53.9 us (8%)
  starting transfers between devices  38.9 us (6%)
  between operations  18.6 us (3%)
    all_to_all x7, waiting for transfers between devices, sent_and_summed(): lax.all_to_all(parts, axis, split_axis=0, concat_axis=0, tiled=True)  53.7 us
    psum x1, blocking collectives, on_device(): table_total = lax.psum(table_grad.T, ('dp', 'seq'))  40.7 us
    all_to_all x7, starting transfers between devices, sent_and_summed(): lax.all_to_all(parts, axis, split_axis=0, concat_axis=0, tiled=True)  30 us
    dot_general x6, matrix products, rows_dot(): jnp.einsum('rd,re->de', left, right, preferred_element_type=jnp.float32)  29 us
    unnamed x299, local copies, waits for them, and re-layouts  21.2 us
    another operation x8, other arithmetic  19.6 us
    another operation x11, local copies, waits for them, and re-layouts  17.2 us
    scatter-add x4, local copies, waits for them, and re-layouts, on_device(): ext_grad.at[0, begin:begin + sub_window]  16.1 us
  transfers between devices with their start and end apart: 19, of which 6 were waited for; matrix products, arithmetic and copies ran while one was open for 51% of the time, Pallas kernels for 0%

commit v1 on v0

v1 whole, which is shorter than its diff:
```python
import functools

import jax
import jax.numpy as jnp
from jax import lax
from jax.experimental import pallas as pl
from jax.experimental.pallas import tpu as pltpu
from jax.sharding import PartitionSpec as P

HD = 64
R = 84
HALO = 128
GP = 256
SUB = 128
EPSILON = 1e-05
MASKED = -1e30
F32 = jnp.float32
BF16 = jnp.bfloat16


def norm_forward(values, gain, shift):
    average = jnp.mean(values, -1, keepdims=True)
    centred = values - average
    variance = jnp.mean(centred * centred, -1, keepdims=True)
    inverse = lax.rsqrt(variance + EPSILON)
    normed = centred * inverse
    return (normed * gain + shift, normed, inverse)


def norm_backward(grad_rows, normed, inverse, gain):
    scaled = grad_rows * gain
    grad_in = inverse * (
        scaled
        - jnp.mean(scaled, -1, keepdims=True)
        - normed * jnp.mean(scaled * normed, -1, keepdims=True)
    )
    return (grad_in, jnp.sum(grad_rows * normed, 0), jnp.sum(grad_rows, 0))


def smooth_gate(values):
    return jax.nn.gelu(values, approximate=True)


def dot_t(left, right):
    return lax.dot_general(left, right, (((1,), (1,)), ((), ())), preferred_element_type=F32)


def dot_n(left, right):
    return lax.dot_general(left, right, (((1,), (0,)), ((), ())), preferred_element_type=F32)


def t_dot(left, right):
    return lax.dot_general(left, right, (((0,), (0,)), ((), ())), preferred_element_type=F32)


def band_bias(table_row, rows, width):
    spread = jnp.broadcast_to(table_row, (rows, width))
    return pltpu.roll(spread, 0, 1, stride=1, stride_axis=0)


def diagonal_sums(rows):
    height, width = rows.shape
    while height > 8:
        height //= 2
        rows = rows[:height] + pltpu.roll(rows[height:], width - height, 1)
    row = lax.broadcasted_iota(jnp.int32, rows.shape, 0)
    for bit in (1, 2, 4):
        rows = jnp.where((row & bit) != 0, pltpu.roll(rows, width - bit, 1), rows)
    return jnp.sum(rows, 0, keepdims=True)


def valid_bias(meta_ref, block, start, width):
    doc_len, seq_index = meta_ref[0], meta_ref[1]
    key_pos = (
        seq_index * block - HALO + start + lax.broadcasted_iota(jnp.int32, (1, width), 1)
    )
    return jnp.where((key_pos >= 0) & (key_pos < doc_len), 0.0, MASKED)


def glob_bias(first, width, count):
    return jnp.where(
        first + lax.broadcasted_iota(jnp.int32, (1, width), 1) < count, 0.0, MASKED
    )


def attend_kernel(dims, meta_ref, tab_ref, q_ref, kx_ref, vx_ref, kg_ref, vg_ref, o_ref, l_ref):
    block, count, quarter = dims
    window = SUB + 2 * HALO
    low_lanes = lax.broadcasted_iota(jnp.int32, (1, 2 * HD), 1) < HD
    scale = HD ** (-0.5)
    kg, vg = kg_ref[...], vg_ref[...]
    every_glob = glob_bias(0, GP, count)
    biases = [band_bias(tab_ref[0, head : head + 1], SUB, window) for head in range(2)]

    def own_half(head, value):
        lanes = low_lanes if head == 0 else ~low_lanes
        return jnp.where(lanes, value, jnp.zeros_like(value))

    for sub in range(block // SUB):
        rows = slice(sub * SUB, (sub + 1) * SUB)
        keys = slice(sub * SUB, sub * SUB + window)
        valid = valid_bias(meta_ref, block, sub * SUB, window)
        query = q_ref[rows] * jnp.asarray(scale, BF16)
        outs = []
        for head in range(2):
            own = own_half(head, query)
            band = dot_t(own, kx_ref[keys]) + (biases[head] + valid)
            glob = dot_t(own, kg) + every_glob
            top = jnp.maximum(
                jnp.max(band, -1, keepdims=True), jnp.max(glob, -1, keepdims=True)
            )
            band_exp = jnp.exp(band - top)
            glob_exp = jnp.exp(glob - top)
            total = jnp.sum(band_exp, -1, keepdims=True) + jnp.sum(glob_exp, -1, keepdims=True)
            mixed = dot_n(band_exp.astype(BF16), vx_ref[keys]) + dot_n(glob_exp.astype(BF16), vg)
            outs.append(mixed / total)
            l_ref[0, rows, head : head + 1] = top + jnp.log(total)
        o_ref[rows] = jnp.where(low_lanes, outs[0], outs[1]).astype(BF16)

    first = meta_ref[1] * quarter
    own_rows = pl.ds(pl.multiple_of(first, quarter), quarter)
    kq, vq = kg_ref[own_rows], vg_ref[own_rows]
    own_keys = slice(HALO, HALO + block)
    valid = valid_bias(meta_ref, block, HALO, block)
    some_glob = glob_bias(first, quarter, count)
    rows = slice(block, block + GP)
    query = q_ref[rows] * jnp.asarray(scale, BF16)
    outs = []
    for head in range(2):
        own = own_half(head, query)
        far = dot_t(own, kx_ref[own_keys]) + valid
        near = dot_t(own, kq) + some_glob
        top = jnp.maximum(jnp.max(far, -1, keepdims=True), jnp.max(near, -1, keepdims=True))
        far_exp = jnp.exp(far - top)
        near_exp = jnp.exp(near - top)
        total = jnp.sum(far_exp, -1, keepdims=True) + jnp.sum(near_exp, -1, keepdims=True)
        mixed = dot_n(far_exp.astype(BF16), vx_ref[own_keys]) + dot_n(near_exp.astype(BF16), vq)
        outs.append(mixed / total)
        l_ref[0, rows, head : head + 1] = top + jnp.log(total)
    o_ref[rows] = jnp.where(low_lanes, outs[0], outs[1]).astype(BF16)


def attend_back_kernel(
    dims,
    meta_ref,
    tab_ref,
    q_ref,
    kx_ref,
    vx_ref,
    kg_ref,
    vg_ref,
    o_ref,
    do_ref,
    dog_ref,
    l_ref,
    lg_ref,
    dq_ref,
    dkx_ref,
    dvx_ref,
    dkg_ref,
    dvg_ref,
    dtab_ref,
    dkg_acc,
    dvg_acc,
):
    block, count, quarter = dims
    window = SUB + 2 * HALO
    low_lanes = lax.broadcasted_iota(jnp.int32, (1, 2 * HD), 1) < HD
    scale = HD ** (-0.5)
    kg, vg = kg_ref[...], vg_ref[...]
    every_glob = glob_bias(0, GP, count)
    biases = [band_bias(tab_ref[0, head : head + 1], SUB, window) for head in range(2)]

    def own_half(head, value):
        lanes = low_lanes if head == 0 else ~low_lanes
        return jnp.where(lanes, value, jnp.zeros_like(value))

    first = meta_ref[1] * quarter
    own_rows = pl.ds(pl.multiple_of(first, quarter), quarter)
    own_keys = slice(HALO, HALO + block)

    dkx_ref[...] = jnp.zeros_like(dkx_ref)
    dvx_ref[...] = jnp.zeros_like(dvx_ref)
    dkg_acc[...] = jnp.zeros_like(dkg_acc)
    dvg_acc[...] = jnp.zeros_like(dvg_acc)
    kq, vq = kg_ref[own_rows], vg_ref[own_rows]
    valid = valid_bias(meta_ref, block, HALO, block)
    some_glob = glob_bias(first, quarter, count)
    query = q_ref[block:] * jnp.asarray(scale, BF16)
    grad_o = dog_ref[...]
    outs, kept = [], []
    for head in range(2):
        own, dog = own_half(head, query), own_half(head, grad_o)
        norm = lg_ref[0, :, head : head + 1]
        delta = lg_ref[0, :, 2 + head : 3 + head]
        far = jnp.exp(dot_t(own, kx_ref[own_keys]) + valid - norm)
        near = jnp.exp(dot_t(own, kq) + some_glob - norm)
        far_ds = (far * (dot_t(dog, vx_ref[own_keys]) - delta)).astype(BF16)
        near_ds = (near * (dot_t(dog, vq) - delta)).astype(BF16)
        outs.append(dot_n(far_ds, kx_ref[own_keys]) + dot_n(near_ds, kq))
        kept.append((own, dog, far.astype(BF16), near.astype(BF16), far_ds, near_ds))
    own, dog, far, near, far_ds, near_ds = (jnp.concatenate(pair, 0) for pair in zip(*kept))
    dq_ref[block:] = (jnp.where(low_lanes, outs[0], outs[1]) * scale).astype(BF16)
    dkx_ref[own_keys] = t_dot(far_ds, own)
    dvx_ref[own_keys] = t_dot(far, dog)
    dkg_acc[own_rows] = t_dot(near_ds, own)
    dvg_acc[own_rows] = t_dot(near, dog)

    table_sum = [jnp.zeros((SUB, window), F32) for _ in range(2)]
    for sub in range(block // SUB):
        rows = slice(sub * SUB, (sub + 1) * SUB)
        keys = slice(sub * SUB, sub * SUB + window)
        valid = valid_bias(meta_ref, block, sub * SUB, window)
        query = q_ref[rows] * jnp.asarray(scale, BF16)
        grad_o = do_ref[rows]
        both = grad_o.astype(F32) * o_ref[rows].astype(F32)
        outs, kept = [], []
        for head in range(2):
            own, dol = own_half(head, query), own_half(head, grad_o)
            norm = l_ref[0, rows, head : head + 1]
            delta = jnp.sum(own_half(head, both), -1, keepdims=True)
            band = jnp.exp(dot_t(own, kx_ref[keys]) + (biases[head] + valid) - norm)
            glob = jnp.exp(dot_t(own, kg) + every_glob - norm)
            band_ds = band * (dot_t(dol, vx_ref[keys]) - delta)
            table_sum[head] += band_ds
            band_ds = band_ds.astype(BF16)
            glob_ds = (glob * (dot_t(dol, vg) - delta)).astype(BF16)
            outs.append(dot_n(band_ds, kx_ref[keys]) + dot_n(glob_ds, kg))
            kept.append((own, dol, band.astype(BF16), glob.astype(BF16), band_ds, glob_ds))
        own, dol, band, glob, band_ds, glob_ds = (
            jnp.concatenate(pair, 0) for pair in zip(*kept)
        )
        dq_ref[rows] = (jnp.where(low_lanes, outs[0], outs[1]) * scale).astype(BF16)
        dkx_ref[keys] += t_dot(band_ds, own)
        dvx_ref[keys] += t_dot(band, dol)
        dkg_acc[...] += t_dot(glob_ds, own)
        dvg_acc[...] += t_dot(glob, dol)
    dkg_ref[...] = dkg_acc[...].astype(BF16)
    dvg_ref[...] = dvg_acc[...].astype(BF16)
    for head in range(2):
        dtab_ref[0, head : head + 1] = diagonal_sums(table_sum[head])


def columns(rows):
    return pl.BlockSpec((rows, 2 * HD), lambda pair: (0, pair))


def per_pair(*dims):
    return pl.BlockSpec((1,) + dims, lambda pair: (pair,) + (0,) * len(dims))


def attend(dims, meta, table, q, kx, vx, kg, vg):
    block = dims[0]
    pairs, width = table.shape[0], q.shape[1]
    window = table.shape[2]
    ext = block + 2 * HALO
    return pl.pallas_call(
        functools.partial(attend_kernel, dims),
        grid=(pairs,),
        in_specs=[
            pl.BlockSpec(memory_space=pltpu.SMEM),
            per_pair(2, window),
            columns(block + GP),
            columns(ext),
            columns(ext),
            columns(GP),
            columns(GP),
        ],
        out_specs=[columns(block + GP), per_pair(block + GP, 2)],
        out_shape=[
            jax.ShapeDtypeStruct((block + GP, width), BF16),
            jax.ShapeDtypeStruct((pairs, block + GP, 2), F32),
        ],
        compiler_params=pltpu.CompilerParams(vmem_limit_bytes=48 * 2**20),
        name="attend",
    )(meta, table, q, kx, vx, kg, vg)


def attend_back(dims, meta, table, q, kx, vx, kg, vg, o, do, dog, l, lg):
    block = dims[0]
    pairs, width = table.shape[0], q.shape[1]
    window = table.shape[2]
    ext = block + 2 * HALO
    return pl.pallas_call(
        functools.partial(attend_back_kernel, dims),
        grid=(pairs,),
        in_specs=[
            pl.BlockSpec(memory_space=pltpu.SMEM),
            per_pair(2, window),
            columns(block + GP),
            columns(ext),
            columns(ext),
            columns(GP),
            columns(GP),
            columns(block),
            columns(block),
            columns(GP),
            per_pair(block, 2),
            per_pair(GP, 4),
        ],
        out_specs=[
            columns(block + GP),
            columns(ext),
            columns(ext),
            columns(GP),
            columns(GP),
            per_pair(2, window),
        ],
        out_shape=[
            jax.ShapeDtypeStruct((block + GP, width), BF16),
            jax.ShapeDtypeStruct((ext, width), F32),
            jax.ShapeDtypeStruct((ext, width), F32),
            jax.ShapeDtypeStruct((GP, width), BF16),
            jax.ShapeDtypeStruct((GP, width), BF16),
            jax.ShapeDtypeStruct((pairs, 2, window), F32),
        ],
        scratch_shapes=[pltpu.VMEM((GP, 2 * HD), F32), pltpu.VMEM((GP, 2 * HD), F32)],
        compiler_params=pltpu.CompilerParams(vmem_limit_bytes=48 * 2**20),
        name="attend_back",
    )(meta, table, q, kx, vx, kg, vg, o, do, dog, l, lg)


def passed_along(value, axis, steps):
    count = lax.axis_size(axis)
    first, last = (max(0, -steps), min(count, count - steps))
    return lax.ppermute(value, axis, [(source, source + steps) for source in range(first, last)])


def matmul(left, right):
    return jnp.dot(left, right, preferred_element_type=F32)


def rows_dot(left, right):
    return jnp.einsum("rd,re->de", left, right, preferred_element_type=F32)


def back_dot(left, right):
    return lax.dot_general(left, right, (((1,), (1,)), ((), ())), preferred_element_type=F32)


def on_device(
    long_input,
    global_input,
    lengths,
    w_query,
    b_query,
    w_key,
    w_value,
    b_value,
    w_out,
    b_out,
    w_inner,
    b_inner,
    w_outer,
    b_outer,
    norm1_gain,
    norm1_shift,
    norm2_gain,
    norm2_shift,
    rel_table,
    long_cotangent,
    global_cotangent,
):
    seq_count = lax.axis_size("seq")
    data_count = lax.axis_size("dp")
    seq_index = lax.axis_index("seq")
    block = long_input.shape[1]
    count = global_input.shape[1]
    width = long_input.shape[2]
    heads = rel_table.shape[1]
    pairs = heads // 2
    labels = 2 * R + 1
    quarter = GP // seq_count
    dims = (block, count, quarter)
    doc_len = lengths[0]
    row_valid = (seq_index * block + jnp.arange(block, dtype=jnp.int32)) < doc_len
    meta = jnp.stack([doc_len, seq_index]).astype(jnp.int32)
    window = SUB + 2 * HALO
    table = jnp.pad(
        rel_table.T,
        ((0, 0), (HALO - R, window - labels - HALO + R)),
        constant_values=MASKED,
    ).reshape(pairs, 2, window)

    glob_x = jnp.pad(global_input[0], ((0, GP - count), (0, 0)))
    glob_dy = jnp.pad(global_cotangent[0], ((0, GP - count), (0, 0)))
    own_glob = lambda a: lax.dynamic_slice_in_dim(a, seq_index * quarter, quarter, 0)
    all_x = jnp.concatenate([long_input[0], glob_x], 0).astype(F32)
    own_x = jnp.concatenate([long_input[0], own_glob(glob_x)], 0).astype(F32)
    normed = norm_forward(all_x, norm1_gain, norm1_shift)[0].astype(BF16)
    keys = matmul(normed, w_key).astype(BF16)
    values = (matmul(normed, w_value) + b_value).astype(BF16)
    queries = (matmul(normed, w_query) + b_query).astype(BF16)

    def extended(rows):
        below = passed_along(rows[block - HALO : block], "seq", 1)
        above = passed_along(rows[:HALO], "seq", -1)
        return jnp.concatenate([below, rows[:block], above], 0)

    kx, vx = extended(keys), extended(values)
    kg, vg = keys[block:], values[block:]
    attended, norms = attend(dims, meta, table, queries, kx, vx, kg, vg)

    def to_owner(part):
        return lax.all_to_all(
            part.reshape(seq_count, quarter, -1), "seq", split_axis=0, concat_axis=0, tiled=True
        )

    part_o = to_owner(attended[block:]).astype(F32).reshape(seq_count, quarter, heads, HD)
    part_l = to_owner(norms[:, block:].transpose(1, 0, 2).reshape(GP, heads))
    top = jnp.max(part_l, 0)
    glob_l = top + jnp.log(jnp.sum(jnp.exp(part_l - top), 0))
    glob_o = jnp.sum(part_o * jnp.exp(part_l - glob_l)[..., None], 0).reshape(quarter, width)
    attn_low = jnp.concatenate([attended[:block], glob_o.astype(BF16)], 0)

    residual_mid = own_x + matmul(attn_low, w_out) + b_out
    normed_two, hat_two, inv_two = norm_forward(residual_mid, norm2_gain, norm2_shift)
    normed_two_low = normed_two.astype(BF16)
    hidden_pre = matmul(normed_two_low, w_inner) + b_inner
    activated, gelu_back = jax.vjp(smooth_gate, hidden_pre)
    activated_low = activated.astype(BF16)
    result = residual_mid + matmul(activated_low, w_outer) + b_outer
    long_result = jnp.where(row_valid[:, None], result[:block], 0.0).astype(BF16)
    grad_y_low = jnp.concatenate(
        [
            jnp.where(row_valid[:, None], long_cotangent[0], jnp.zeros_like(long_cotangent[0])),
            own_glob(glob_dy),
        ],
        0,
    )
    grad_y = grad_y_low.astype(F32)
    grad_b_outer = jnp.sum(grad_y, 0)
    grad_w_outer = rows_dot(activated_low, grad_y_low)
    (grad_hidden,) = gelu_back(back_dot(grad_y_low, w_outer))
    grad_b_inner = jnp.sum(grad_hidden, 0)
    hidden_low = grad_hidden.astype(BF16)
    grad_w_inner = rows_dot(normed_two_low, hidden_low)
    grad_from_two, grad_gain_two, grad_shift_two = norm_backward(
        back_dot(hidden_low, w_inner), hat_two, inv_two, norm2_gain
    )
    grad_mid = grad_y + grad_from_two
    grad_b_out = jnp.sum(grad_mid, 0)
    grad_mid_low = grad_mid.astype(BF16)
    grad_w_out = rows_dot(attn_low, grad_mid_low)
    grad_attn = back_dot(grad_mid_low, w_out).astype(BF16)

    glob_do = grad_attn[block:]
    glob_delta = jnp.sum((glob_do.astype(F32) * glob_o).reshape(quarter, heads, HD), -1)
    every_do = lax.all_gather(glob_do, "seq", axis=0, tiled=True)
    every_ld = lax.all_gather(
        jnp.concatenate(
            [glob_l.reshape(quarter, pairs, 2), glob_delta.reshape(quarter, pairs, 2)], -1
        ),
        "seq",
        axis=0,
        tiled=True,
    ).transpose(1, 0, 2)
    dq, dkx, dvx, dkg, dvg, dtab = attend_back(
        dims,
        meta,
        table,
        queries,
        kx,
        vx,
        kg,
        vg,
        attended[:block],
        grad_attn[:block],
        every_do,
        norms[:, :block],
        every_ld,
    )
    glob_sum = lax.psum_scatter(
        jnp.concatenate([dq[block:], dkg, dvg], 1), "seq", scatter_dimension=0, tiled=True
    )

    def joined(ext):
        from_above = passed_along(ext[:HALO].astype(BF16), "seq", -1).astype(F32)
        from_below = passed_along(ext[HALO + block :].astype(BF16), "seq", 1).astype(F32)
        own = ext[HALO : HALO + block]
        return jnp.concatenate(
            [
                own[:HALO] + from_below,
                own[HALO : block - HALO],
                own[block - HALO :] + from_above,
            ],
            0,
        ).astype(BF16)

    query_low = jnp.concatenate([dq[:block], glob_sum[:, :width]], 0)
    key_low = jnp.concatenate([joined(dkx), glob_sum[:, width : 2 * width]], 0)
    value_low = jnp.concatenate([joined(dvx), glob_sum[:, 2 * width :]], 0)
    own_normed, hat_one, inv_one = norm_forward(own_x, norm1_gain, norm1_shift)
    own_normed = own_normed.astype(BF16)
    grad_b_query = jnp.sum(query_low.astype(F32), 0)
    grad_b_value = jnp.sum(value_low.astype(F32), 0)
    grad_w_query = rows_dot(own_normed, query_low)
    grad_w_key = rows_dot(own_normed, key_low)
    grad_w_value = rows_dot(own_normed, value_low)
    grad_normed_one = (
        back_dot(query_low, w_query) + back_dot(key_low, w_key) + back_dot(value_low, w_value)
    )
    grad_from_one, grad_gain_one, grad_shift_one = norm_backward(
        grad_normed_one, hat_one, inv_one, norm1_gain
    )
    grad_x = grad_mid + grad_from_one

    def summed(part):
        return lax.psum_scatter(
            part.astype(BF16), ("dp", "seq"), scatter_dimension=0, tiled=True
        ).astype(F32)

    devices = data_count * seq_count
    piece = width // devices
    vectors = (
        grad_b_query,
        grad_b_value,
        grad_b_out,
        grad_b_inner,
        grad_b_outer,
        grad_gain_one,
        grad_shift_one,
        grad_gain_two,
        grad_shift_two,
    )
    small = summed(jnp.concatenate([v.reshape(devices, -1) for v in vectors], 1))[0]
    pieces, at = [], 0
    for vector in vectors:
        length = vector.shape[0] // devices
        pieces.append(small[at : at + length])
        at += length
    g_b_query, g_b_value, g_b_out, g_b_inner, g_b_outer, g_g1, g_s1, g_g2, g_s2 = pieces
    turned = dtab.reshape(heads, window)[:, HALO - R : HALO - R + labels]
    table_total = lax.psum(turned.T, ("dp", "seq"))
    glob_out = lax.all_gather(result[block:].astype(BF16), "seq", axis=0, tiled=True)[:count]
    glob_grad = lax.all_gather(grad_x[block:], "seq", axis=0, tiled=True)[:count]
    return (
        long_result[None],
        glob_out[None],
        grad_x[:block][None],
        glob_grad[None],
        summed(grad_w_query),
        g_b_query,
        summed(grad_w_key),
        summed(grad_w_value),
        g_b_value,
        summed(grad_w_out),
        g_b_out,
        summed(grad_w_inner),
        g_b_inner,
        summed(grad_w_outer),
        g_b_outer,
        g_g1,
        g_s1,
        g_g2,
        g_s2,
        table_total,
    )


def solution(mesh):
    rows, whole = P("dp", "seq", None), P("dp", None, None)
    matrix, vector = P(("dp", "seq"), None), P(("dp", "seq"))
    return jax.shard_map(
        on_device,
        mesh=mesh,
        in_specs=(rows, whole, P("dp")) + (P(),) * 16 + (rows, whole),
        out_specs=(
            rows,
            whole,
            rows,
            whole,
            matrix,
            vector,
            matrix,
            matrix,
            vector,
            matrix,
            vector,
            matrix,
            vector,
            matrix,
            vector,
            vector,
            vector,
            vector,
            vector,
            P(),
        ),
        check_vma=False,
    )
```

time: 675 us -> 845 us (1.25)
  waiting for transfers between devices: 53.9 us -> 480 us
  local copies, waits for them, and re-layouts: 216 us -> 40.4 us
  matrix products: 170 us -> 67.1 us
  Pallas kernels: 0 us -> 53.2 us
  other arithmetic: 87.2 us -> 38.3 us
  blocking collectives: 79.5 us -> 114 us
  starting transfers between devices: 38.9 us -> 27.3 us
    reduce_scatter x6 -> x7, waiting for transfers between devices: 0.04 us -> 474 us  [the longest x6 462 us: summed(): lax.psum_scatter(part.astype(BF16), ('dp', 'seq'), scatter_dimension=0, t...]
    dot_general x42 -> x18, matrix products: 170 us -> 67.1 us  [the longest x6 31.1 us: rows_dot(): return jnp.einsum('rd,re->de', left, right, preferred_element_type=F32)]
    pallas_call x0 -> x2, Pallas kernels: none -> 53.2 us  [the longest x1 29.6 us: attend_back(): pl.pallas_call(functools.partial(attend_back_kernel, dims), grid=(pairs,)...]
    all_to_all x7 -> x2, waiting for transfers between devices: 53.7 us -> 1.68 us  [to_owner(): lax.all_to_all(part.reshape(seq_count, quarter, -1), 'seq', split_axis=0,...]
    slice x34 -> x21, local copies, waits for them, and re-layouts: 44 us -> 7.6 us  [the longest x2 1.69 us: extended(): below = passed_along(rows[block - HALO:block], 'seq', 1)]
    reshape x10 -> x13, local copies, waits for them, and re-layouts: 42.9 us -> 6.91 us  [the longest x9 4.42 us: on_device(): v.reshape(devices, -1)]
    unnamed x1, blocking collectives: 13.3 us -> 39.3 us
    another operation x18 -> x2, local copies, waits for them, and re-layouts: 24.5 us -> 0.1 us  [to_owner(): part.reshape(seq_count, quarter, -1)]
  transfers between devices with their start and end apart: 19 -> 17, of which waited for: 6 -> 11; matrix products, arithmetic and copies ran while one was open for 51% -> 11% of each run, Pallas kernels for 0% -> 0%
where the time goes in v1:
time: 845 us; the launch traced here: 837 us
  waiting for transfers between devices  480 us (57%)
  blocking collectives  114 us (13%)
  matrix products  67.1 us (8%)
  Pallas kernels  53.2 us (6%)
  local copies, waits for them, and re-layouts  40.4 us (5%)
  other arithmetic  38.3 us (5%)
  starting transfers between devices  27.3 us (3%)
  between operations  16.5 us (2%)
    reduce_scatter x6, waiting for transfers between devices, summed(): lax.psum_scatter(part.astype(BF16), ('dp', 'seq'), scatter_dimension=0, t...  462 us
    psum x1, blocking collectives, on_device(): table_total = lax.psum(turned.T, ('dp', 'seq'))  43.4 us
    unnamed x1, blocking collectives  39.3 us
    dot_general x6, matrix products, rows_dot(): return jnp.einsum('rd,re->de', left, right, preferred_element_type=F32)  31.1 us
    pallas_call x1, Pallas kernels, attend_back(): pl.pallas_call(functools.partial(attend_back_kernel, dims), grid=(pairs,)...  29.6 us
    pallas_call x1, Pallas kernels, attend(): pl.pallas_call(functools.partial(attend_kernel, dims), grid=(pairs,), in_...  23.6 us
    dot_general x6, matrix products, back_dot(): lax.dot_general(left, right, (((1,), (1,)), ((), ())), preferred_element_...  19.8 us
    ppermute x8, starting transfers between devices, passed_along(): lax.ppermute(value, axis, [(source, source + steps) for source in range(f...  17.6 us
  transfers between devices with their start and end apart: 17, of which 11 were waited for; matrix products, arithmetic and copies ran while one was open for 11% of the time, Pallas kernels for 0%

profile of v1, /device:TPU:0, one launch (start us, length us, event | category | flops | bytes accessed | tf_op | source)
XLA Modules:
  0.0 836.8 jit_solution(13236409600360183180)
XLA Ops:
  19.1 5.0 collective-permute-start.2
  27.7 3.7 add_convert_fusion.1.q_ref
  38.8 23.6 %attend.1 = (bf16[768,768]{1,0:T(8,128)(2,1)S(1)}, f32[6,768,2]{2,1,0:T(8,128)}) custom-call(s32[2]{0:T(128)S(1)} %pad_add_fusion.meta_ref, f32[6,2,384]{2,1,0:T(2,128)S(1)} %reshape.184.tab_ref, bf16[768,768]{1,0:T(8,128)(2,1)S(1)} %copy-done.3, bf16[768,768]{1,0:T(8,128)(2,1)S(1)} %pad_maximum_fusion.1.kx_ref, ...), custom_call_target="tpu_custom_call" | custom-call | tf_op jit(solution)/shard_map/attend/pallas_call | solution.py:257
  64.6 4.6 all-to-all-start.1
  73.1 4.1 all-to-all-start
  92.2 4.5 add_add_fusion.1
  99.5 9.3 %fusion.64 = (bf16[3072]{0:T(1024)(128)(2,1)}, bf16[576,3072]{1,0:T(8,128)(2,1)S(1)}) fusion(f32[576,3072]{1,0:T(8,128)S(1)} %fusion.47, f32[3072]{0:T(1024)S(1)} %copy-done.82, bf16[3072,768]{1,0:T(8,128)(2,1)S(1)} %bitcast.89, bf16[64,768]{1,0:T(8,128)(2,1)S(1)} %copy-done.37, bf16[512,768]{1,0:T(8,128)(2,1)S(1)} %get-tuple-element.109), kind=kOutput, calls=%fused_computation.143 | convolution fusion | flops 2758603776 | bytes 16238592 | tf_op jit(solution)/shard_map/dot_general | solution.py:338
  108.8 3.9 multiply_reduce_fusion
  115.8 6.7 all_gather.13.dog_ref
  129.2 8.9 %all_gather.14 = f32[256,6,4]{2,0,1:T(8,128)S(1)} all-gather(f32[64,6,4]{2,0,1:T(8,128)} %copy.51), channel_id=1, replica_groups=mesh['dp'=8,'seq'=4] {'seq'}, dimensions={0}, use_global_device_ids=true | all-gather | bytes 30720 | tf_op jit(solution)/shard_map/all_gather | solution.py:450
  139.8 29.6 %attend_back.1 = (bf16[768,768]{1,0:T(8,128)(2,1)S(1)}, f32[768,768]{1,0:T(8,128)}, f32[768,768]{1,0:T(8,128)}, bf16[256,768]{1,0:T(8,128)(2,1)S(1)}, bf16[256,7...) custom-call(s32[2]{0:T(128)S(1)} %pad_add_fusion.meta_ref, f32[6,2,384]{2,1,0:T(2,128)S(1)} %copy-done.12, ...), custom_call_target="tpu_custom_call" | custom-call | tf_op jit(solution)/shard_map/attend_back/pallas_call | solution.py:284
  186.2 12.4 %reduce-scatter.8.cloned.1.call-done = bf16[64,2304]{1,0:T(8,128)(2,1)} async-done(((bf16[256,2304]{1,0:T(8,128)(2,1)}), bf16[64,2304]{1,0:T(8,128)(2,1)}) %reduce-scatter.8.cloned.1.call-update) | async-done | bytes 294928 | tf_op jit(solution)/shard_map/reduce_scatter | solution.py:473
  220.0 10.4 %convolution_convert_fusion = bf16[3072,768]{1,0:T(8,128)(2,1)} fusion(bf16[64,768]{1,0:T(8,128)(2,1)S(1)} %copy-done.38, bf16[512,768]{1,0:T(8,128)(2,1)S(1)} %copy-done.23, f32[576,3072]{1,0:T(8,128)} %copy-done.92, f32[3072]{0:T(1024)S(1)} %copy-done.83), kind=kOutput, calls=%fused_computation.9 | convolution fusion | flops 2739732480 | bytes 12693504 | tf_op jit(solution)/shard_map/rd,re->de/dot_general | solution.py:334
  231.1 8.8 %convolution_convert_fusion.1 = bf16[768,3072]{1,0:T(8,128)(2,1)} fusion(bf16[576,3072]{1,0:T(8,128)(2,1)} %copy-done.93, f32[576,768]{1,0:T(8,128)} %copy-done.18, f32[768]{0:T(1024)S(1)} %copy-done.91, f32[768]{0:T(1024)S(1)} %copy-done.73, f32[576]{0:T(1024)S(1)} %copy-done.60, f32[576]{0:T(1024)S(1)} %copy-done.52), kind=kOutput, calls=%fused_computation.10 | convolution fusion | flops 2722480128 | bytes 10037760 | tf_op jit(solution)/shard_map/rd,re->de/dot_general | solution.py:334
  243.7 43.4 %psum.7 = f32[169,12]{0,1:T(8,128)} all-reduce(f32[169,12]{0,1:T(8,128)S(1)} %slice_bitcast_fusion.4), channel_id=1, replica_groups=mesh['dp'=8,'seq'=4] {'dp','seq'}, use_global_device_ids=true, to_apply=%region_31.32 | all-reduce | flops 2028 | bytes 16224 | tf_op jit(solution)/shard_map/psum | solution.py:534
  287.0 7.2 all_gather.12
  295.0 5.7 reduce-scatter.16.cloned.1.call-done
  313.7 8.7 %all_gather.15 = f32[256,768]{1,0:T(8,128)S(1)} all-gather(f32[64,768]{1,0:T(8,128)S(1)} %slice.255), channel_id=1, replica_groups=mesh['dp'=8,'seq'=4] {'seq'}, dimensions={0}, use_global_device_ids=true | all-gather | bytes 983040 | tf_op jit(solution)/shard_map/all_gather | solution.py:536
  324.2 39.3 %all-reduce.3 = bf16[32,288]{1,0:T(8,128)(2,1)S(1)} all-reduce(bf16[32,288]{1,0:T(8,128)(2,1)S(1)} %concatenate.54), channel_id=4, replica_groups=mesh['dp'=8,'seq'=4] {'dp','seq'}, use_global_device_ids=true, to_apply=%region_25.26.clone | all-reduce | flops 9216 | bytes 36864
  366.0 35.9 %reduce-scatter.14.cloned.1.call-done = bf16[24,768]{1,0:T(8,128)(2,1)} async-done(((bf16[768,768]{1,0:T(8,128)(2,1)}), bf16[24,768]{1,0:T(8,128)(2,1)}) %reduce-scatter.14.cloned.1.call-update) | async-done | bytes 36880 | tf_op jit(solution)/shard_map/reduce_scatter | solution.py:509
  403.3 99.6 %reduce-scatter.12.cloned.1.call-done = bf16[24,768]{1,0:T(8,128)(2,1)} async-done(((bf16[768,768]{1,0:T(8,128)(2,1)}), bf16[24,768]{1,0:T(8,128)(2,1)}) %reduce-scatter.12.cloned.1.call-update) | async-done | bytes 36880 | tf_op jit(solution)/shard_map/reduce_scatter | solution.py:509
  504.3 99.6 %reduce-scatter.10.cloned.1.call-done = bf16[24,768]{1,0:T(8,128)(2,1)} async-done(((bf16[768,768]{1,0:T(8,128)(2,1)}), bf16[24,768]{1,0:T(8,128)(2,1)}) %reduce-scatter.10.cloned.1.call-update) | async-done | bytes 36880 | tf_op jit(solution)/shard_map/reduce_scatter | solution.py:509
  605.4 110.9 %reduce-scatter.20.cloned.1.call-done = bf16[96,768]{1,0:T(8,128)(2,1)} async-done(((bf16[3072,768]{1,0:T(8,128)(2,1)}), bf16[96,768]{1,0:T(8,128)(2,1)}) %reduce-scatter.20.cloned.1.call-update) | async-done | bytes 147472 | tf_op jit(solution)/shard_map/reduce_scatter | solution.py:509
  718.0 109.9 %reduce-scatter.18.cloned.1.call-done = bf16[24,3072]{1,0:T(8,128)(2,1)} async-done(((bf16[768,3072]{1,0:T(8,128)(2,1)}), bf16[24,3072]{1,0:T(8,128)(2,1)}) %reduce-scatter.18.cloned.1.call-update) | async-done | bytes 147472 | tf_op jit(solution)/shard_map/reduce_scatter | solution.py:509
  (347 shorter events, 124.4 us)
Async XLA Ops:
  12.5 22.8 %collective-permute-start = (bf16[128,768]{1,0:T(8,128)(2,1)}, bf16[128,768]{1,0:T(8,128)(2,1)}, u32[]{:S(2)}, u32[]{:S(2)}) collective-permute-start(bf16[128,768]{1,0:T(8,128)(2,1)} %get-tuple-element.130), channel_id=1, source_target_pairs={{0,1},{1,2},{2,3},{4,5},{5,6},{6,7},{8,9},{9,10},{10,11},{12,13},{... | collective-permute-start | bytes 589832 | tf_op jit(solution)/shard_map/ppermute | solution.py:326
  15.6 19.7 %collective-permute-start.1 = (bf16[128,768]{1,0:T(8,128)(2,1)}, bf16[128,768]{1,0:T(8,128)(2,1)}, u32[]{:S(2)}, u32[]{:S(2)}) collective-permute-start(bf16[128,768]{1,0:T(8,128)(2,1)} %get-tuple-element.131), channel_id=1, source_target_pairs={{1,0},{2,1},{3,2},{5,4},{6,5},{7,6},{9,8},{10,9},{11,10},{13,12},{... | collective-permute-start | bytes 589832 | tf_op jit(solution)/shard_map/ppermute | solution.py:326
  19.1 17.6 %collective-permute-start.2 = (bf16[128,768]{1,0:T(8,128)(2,1)}, bf16[128,768]{1,0:T(8,128)(2,1)}, u32[]{:S(2)}, u32[]{:S(2)}) collective-permute-start(bf16[128,768]{1,0:T(8,128)(2,1)} %get-tuple-element.128), channel_id=1, source_target_pairs={{0,1},{1,2},{2,3},{4,5},{5,6},{6,7},{8,9},{9,10},{10,11},{12,13},{... | collective-permute-start | bytes 589832 | tf_op jit(solution)/shard_map/ppermute | solution.py:326
  24.1 12.6 %collective-permute-start.3 = (bf16[128,768]{1,0:T(8,128)(2,1)}, bf16[128,768]{1,0:T(8,128)(2,1)}, u32[]{:S(2)}, u32[]{:S(2)}) collective-permute-start(bf16[128,768]{1,0:T(8,128)(2,1)} %get-tuple-element.129), channel_id=1, source_target_pairs={{1,0},{2,1},{3,2},{5,4},{6,5},{7,6},{9,8},{10,9},{11,10},{13,12},{... | collective-permute-start | bytes 589832 | tf_op jit(solution)/shard_map/ppermute | solution.py:326
  64.6 8.4 %all-to-all-start.1 = ((f32[4,1,768]{2,1,0:T(1,128)}), f32[4,1,768]{2,1,0:T(1,128)S(1)}, u32[]{:S(2)}, u32[]{:S(2)}) async-start(f32[4,1,768]{2,1,0:T(1,128)} %reshape.198), calls=%async_computation.1 | async-start | bytes 24576 | tf_op jit(solution)/shard_map/all_to_all | solution.py:405
  73.1 11.6 %all-to-all-start = ((bf16[4,64,768]{2,1,0:T(8,128)(2,1)}), bf16[4,64,768]{2,1,0:T(8,128)(2,1)}, u32[]{:S(2)}, u32[]{:S(2)}) async-start(bf16[4,64,768]{2,1,0:T(8,128)(2,1)} %bitcast.5), calls=%async_computation | async-start | bytes 786432 | tf_op jit(solution)/shard_map/all_to_all | solution.py:405
  77.2 121.4 %reduce-scatter.8.cloned.1.call-start = ((), (), s32[]{:S(2)}) async-start(), calls=%async_computation.9 | async-start | bytes 1474560 | tf_op jit(solution)/shard_map/reduce_scatter | solution.py:473
  171.7 129.0 %reduce-scatter.16.cloned.1.call-start = ((), (), s32[]{:S(2)}) async-start(), calls=%async_computation.13 | async-start | bytes 1216512 | tf_op jit(solution)/shard_map/reduce_scatter | solution.py:509
  175.9 226.0 %reduce-scatter.14.cloned.1.call-start = ((), (), s32[]{:S(2)}) async-start(), calls=%async_computation.12 | async-start | bytes 1216512 | tf_op jit(solution)/shard_map/reduce_scatter | solution.py:509
  178.2 4.4 collective-permute-start.6
  180.5 3.9 collective-permute-start.7
  203.3 299.6 %reduce-scatter.12.cloned.1.call-start = ((), (), s32[]{:S(2)}) async-start(), calls=%async_computation.11 | async-start | bytes 1216512 | tf_op jit(solution)/shard_map/reduce_scatter | solution.py:509
  205.2 3.1 collective-permute-start.4
  206.9 3.4 collective-permute-start.5
  214.8 389.2 %reduce-scatter.10.cloned.1.call-start = ((), (), s32[]{:S(2)}) async-start(), calls=%async_computation.10 | async-start | bytes 1216512 | tf_op jit(solution)/shard_map/reduce_scatter | solution.py:509
  219.9 496.4 %reduce-scatter.20.cloned.1.call-start = ((), (), s32[]{:S(2)}) async-start(), calls=%async_computation.15 | async-start | bytes 4866048 | tf_op jit(solution)/shard_map/reduce_scatter | solution.py:509
  230.4 597.5 %reduce-scatter.18.cloned.1.call-start = ((), (), s32[]{:S(2)}) async-start(), calls=%async_computation.14 | async-start | bytes 4866048 | tf_op jit(solution)/shard_map/reduce_scatter | solution.py:509
  240.1 62.8 %copy-start.65 = (bf16[768]{0:T(1024)(128)(2,1)S(1)}, bf16[768]{0:T(1024)(128)(2,1)}, u32[]{:S(2)}) copy-start(bf16[768]{0:T(1024)(128)(2,1)} %get-tuple-element.120) | copy-start | bytes 4612
  240.1 62.8 %copy-start.66 = (bf16[768]{0:T(1024)(128)(2,1)S(1)}, bf16[768]{0:T(1024)(128)(2,1)}, u32[]{:S(2)}) copy-start(bf16[768]{0:T(1024)(128)(2,1)} %get-tuple-element.112) | copy-start | bytes 4612
  240.1 62.7 %copy-start.67 = (bf16[768]{0:T(1024)(128)(2,1)S(1)}, bf16[768]{0:T(1024)(128)(2,1)}, u32[]{:S(2)}) copy-start(bf16[768]{0:T(1024)(128)(2,1)} %get-tuple-element.116) | copy-start | bytes 4612
  240.1 63.4 %copy-start.36 = (bf16[256,768]{1,0:T(8,128)(2,1)S(1)}, bf16[256,768]{1,0:T(8,128)(2,1)}, u32[]{:S(2)}) copy-start(bf16[256,768]{1,0:T(8,128)(2,1)} %copy-done.35) | copy-start | bytes 1179652
  240.1 63.4 %copy-start.43 = (bf16[128,768]{1,0:T(8,128)(2,1)S(1)}, bf16[128,768]{1,0:T(8,128)(2,1)}, u32[]{:S(2)}) copy-start(bf16[128,768]{1,0:T(8,128)(2,1)} %copy-done.42) | copy-start | bytes 589828
  240.1 63.4 %copy-start.45 = (bf16[128,768]{1,0:T(8,128)(2,1)S(1)}, bf16[128,768]{1,0:T(8,128)(2,1)}, u32[]{:S(2)}) copy-start(bf16[128,768]{1,0:T(8,128)(2,1)} %copy-done.44) | copy-start | bytes 589828
  240.1 63.4 %copy-start.48 = (bf16[64,768]{1,0:T(8,128)(2,1)S(1)}, bf16[64,768]{1,0:T(8,128)(2,1)}, u32[]{:S(2)}) copy-start(bf16[64,768]{1,0:T(8,128)(2,1)} %get-tuple-element.133) | copy-start | bytes 294916
  (93 other events, 810.8 us)
Sparse Core Ops, SparseCore 0:
  171.8 26.7 reduce-scatter.7
  204.5 96.1 reduce-scatter.15
  306.6 95.2 reduce-scatter.13
  407.6 95.2 reduce-scatter.11
  508.7 95.2 reduce-scatter.9
  610.2 106.0 reduce-scatter.19
  721.8 106.0 reduce-scatter.17
